TPU v7x, 256 devices: a whole 4x4x8 slice. The times are simulated.
256 devices in a mesh: dp: 32 (over z_hi, x, y), param: 8 (over z_lo, core).
Axes of the slice: x: 4, y: 4, z: 8 (z_hi: 2, z_lo: 4; z = z_hi * 4 + z_lo), core: 2. Of those that a mesh axis runs over, the one named last changes fastest.
Arguments:
- query_grads: bfloat16 [32, 1280, 1280], P('dp', 'param'), may hold values from -6 to 6
- in_inverse: bfloat16 [1280, 1280], replicated, may hold values from -8.5 to 8.5
- out_inverse: bfloat16 [1280, 1280], replicated, may hold values from -8.5 to 8.5
- activations: bfloat16 [2048, 64, 1280], P('dp', 'param'), may hold values from -6 to 6
- errors: bfloat16 [2048, 64, 1280], P('dp', None, 'param'), may hold values from -6 to 6
Outputs:
- scores: float32 [2048, 32], P(('dp', 'param'))
All inputs are finite; a program needn't handle non-finite values.
Results may differ from a plain program's by a relative error of at most 0.0049.
Values may be sent and summed in bfloat16 or wider, within the bound.
A program may use at most 128 MiB of HBM per device.

v0:
```python
import math

import jax
import jax.numpy as jnp
from jax import lax
from jax.sharding import PartitionSpec as P


def per_device(query_grads, in_inverse, out_inverse, activations, errors):
    channels = in_inverse.shape[0]
    block_out = query_grads.shape[1]
    my_block = lax.axis_index("param")
    all_acts = lax.all_gather(activations, "param", axis=1, tiled=True)
    positions = all_acts.shape[1]
    mixed_in = jnp.einsum(
        "qoi,ij->qoj", query_grads, in_inverse, preferred_element_type=jnp.float32
    ).astype(jnp.bfloat16)
    mixed_full = lax.all_gather(mixed_in, "param", axis=1, tiled=True)
    my_rows = lax.dynamic_slice_in_dim(out_inverse, my_block * block_out, block_out, 0)
    preconditioned = jnp.einsum(
        "ko,qoj->qkj", my_rows, mixed_full, preferred_element_type=jnp.float32
    ).astype(jnp.bfloat16)
    all_queries = lax.all_gather(preconditioned, "dp", axis=0, tiled=True)
    factor = 1.0 / (channels * math.sqrt(positions))
    images = errors.shape[0]
    err_blocks = errors.reshape(images // 16, 16, positions, block_out)
    act_blocks = all_acts.reshape(images // 16, 16, positions, channels)

    def score_block(pair):
        err_part, act_part = pair
        example_grad = jnp.einsum(
            "npo,npi->noi", err_part, act_part, preferred_element_type=jnp.float32
        ).astype(jnp.bfloat16)
        return (
            jnp.einsum("noi,qoi->nq", example_grad, all_queries, preferred_element_type=jnp.float32)
            * factor
        )

    partial_scores = lax.map(score_block, (err_blocks, act_blocks)).reshape(
        images, all_queries.shape[0]
    )
    totals = lax.psum(partial_scores, "param")
    share = images // lax.axis_size("param")
    return lax.dynamic_slice_in_dim(totals, my_block * share, share, 0)


def solution(mesh):
    return jax.shard_map(
        per_device,
        mesh=mesh,
        in_specs=(P("dp", "param", None), P(), P(), P("dp", "param", None), P("dp", None, "param")),
        out_specs=P(("dp", "param"), None),
        check_vma=False,
    )
```

profile of v0, /device:TPU:1, one launch (start us, length us, event | category | flops | bytes accessed | tf_op | source)
XLA Modules:
  0.0 492.1 jit_solution(6575742822701330500)
XLA Ops:
  6.5 0.0 copy-start
  6.5 1.9 copy-done
  8.5 2.5 convolution_convert_fusion.1
  10.9 0.0 all-gather.9.cloned.1.call-update
  11.0 0.0 all-gather.7.cloned.1.call-start
  11.0 47.6 %all-gather.9.cloned.1.call-done = bf16[1280,1280]{1,0:T(8,128)(2,1)} async-done(((bf16[160,1280]{1,0:T(8,128)(2,1)}), bf16[1280,1280]{1,0:T(8,128)(2,1)}) %all-gather.9.cloned.1.call-update) | async-done | bytes 3276816 | tf_op jit(solution)/shard_map/all_gather | solution.py:18
  58.6 3.5 fusion.11
  62.2 0.0 all-gather.7.cloned.1.call-update
  62.2 0.0 all-gather.5.cloned.1.call-start
  62.2 0.7 all-gather.5.cloned.1.call-update
  62.9 205.8 %all-gather.7.cloned.1.call-done = bf16[32,160,1280]{2,1,0:T(8,128)(2,1)} async-done(((bf16[1,160,1280]{2,1,0:T(8,128)(2,1)}), bf16[32,160,1280]{2,1,0:T(8,128)(2,1)}) %all-gather.7.cloned.1.call-update) | async-done | bytes 13107216 | tf_op jit(solution)/shard_map/all_gather | solution.py:23
  268.8 29.0 %copy.7 = bf16[32,160,1280]{2,0,1:T(8,128)(2,1)} copy(bf16[32,160,1280]{2,1,0:T(8,128)(2,1)} %all-gather.7.cloned.1.call-done) | data formatting | bytes 26214400 | tf_op jit(solution)/shard_map/while | solution.py:39
  297.7 79.2 %all-gather.5.cloned.1.call-done = bf16[64,64,1280]{2,1,0:T(8,128)(2,1)} async-done(((bf16[64,8,1280]{2,1,0:T(8,128)(2,1)}), bf16[64,64,1280]{2,1,0:T(8,128)(2,1)}) %all-gather.5.cloned.1.call-update) | async-done | bytes 10485776 | tf_op jit(solution)/shard_map/all_gather | solution.py:13
  376.9 83.2 %while.10 = (s32[]{:T(128)}, f32[4,16,32]{2,1,0:T(8,128)S(1)}, bf16[4,16,64,160]{3,2,1,0:T(8,128)(2,1)}, bf16[4,16,64,1280]{3,2,1,0:T(8,128)(2,1)}, bf16[32,160,1280]{2,0,1:T(8,128)(2,1)}, /*index=5*/s32[]{:T(128)}) while((s32[]{:T(128)}, f32[4,16,32]{2,1,0:T(8,128)S(1)}, bf16[4,16,64,160]{3,2,1,0:T(8,128)(2,1)}, ...), condition=%wide.region_1.2_spmd, body=%wide.region_0.1_spmd.sunk | while | flops 629146112 | bytes 29369416 | solution.py:39
  376.9 6.5 %fusion.26 = bf16[16,160,1280]{2,1,0:T(8,128)(2,1)} fusion(bf16[4,16,64,1280]{3,2,1,0:T(8,128)(2,1)} %get-tuple-element.99, s32[]{:T(128)} %get-tuple-element.90, bf16[4,16,64,160]{3,2,1,0:T(8,128)(2,1)} %get-tuple-element.98), kind=kOutput, calls=%fused_computation.2.clone.1 | convolution fusion | flops 419430400 | bytes 9700352 | tf_op jit(solution)/shard_map/while/body/eval_jaxpr/npo,npi->noi/dot_general | solution.py:31
  383.4 14.3 %fusion.27 = f32[4,16,32]{2,1,0:T(8,128)S(1)} fusion(f32[4,16,32]{2,1,0:T(8,128)S(1)} %get-tuple-element.91, s32[]{:T(128)} %get-tuple-element.90, bf16[32,160,1280]{2,0,1:T(8,128)(2,1)} %get-tuple-element.100, bf16[16,160,1280]{2,1,0:T(8,128)(2,1)} %fusion.26), kind=kOutput, calls=%fused_computation.8.clone.1 | convolution fusion | flops 209715712 | bytes 19668996 | tf_op jit(solution)/shard_map/while/body/eval_jaxpr/noi,qoi->nq/dot_general | solution.py:35
  397.7 6.5 %fusion.26 = bf16[16,160,1280]{2,1,0:T(8,128)(2,1)} fusion(bf16[4,16,64,1280]{3,2,1,0:T(8,128)(2,1)} %get-tuple-element.99, s32[]{:T(128)} %get-tuple-element.90, bf16[4,16,64,160]{3,2,1,0:T(8,128)(2,1)} %get-tuple-element.98), kind=kOutput, calls=%fused_computation.2.clone.1 | convolution fusion | flops 419430400 | bytes 9700352 | tf_op jit(solution)/shard_map/while/body/eval_jaxpr/npo,npi->noi/dot_general | solution.py:31
  404.2 14.3 %fusion.27 = f32[4,16,32]{2,1,0:T(8,128)S(1)} fusion(f32[4,16,32]{2,1,0:T(8,128)S(1)} %get-tuple-element.91, s32[]{:T(128)} %get-tuple-element.90, bf16[32,160,1280]{2,0,1:T(8,128)(2,1)} %get-tuple-element.100, bf16[16,160,1280]{2,1,0:T(8,128)(2,1)} %fusion.26), kind=kOutput, calls=%fused_computation.8.clone.1 | convolution fusion | flops 209715712 | bytes 19668996 | tf_op jit(solution)/shard_map/while/body/eval_jaxpr/noi,qoi->nq/dot_general | solution.py:35
  418.5 6.5 %fusion.26 = bf16[16,160,1280]{2,1,0:T(8,128)(2,1)} fusion(bf16[4,16,64,1280]{3,2,1,0:T(8,128)(2,1)} %get-tuple-element.99, s32[]{:T(128)} %get-tuple-element.90, bf16[4,16,64,160]{3,2,1,0:T(8,128)(2,1)} %get-tuple-element.98), kind=kOutput, calls=%fused_computation.2.clone.1 | convolution fusion | flops 419430400 | bytes 9700352 | tf_op jit(solution)/shard_map/while/body/eval_jaxpr/npo,npi->noi/dot_general | solution.py:31
  425.0 14.3 %fusion.27 = f32[4,16,32]{2,1,0:T(8,128)S(1)} fusion(f32[4,16,32]{2,1,0:T(8,128)S(1)} %get-tuple-element.91, s32[]{:T(128)} %get-tuple-element.90, bf16[32,160,1280]{2,0,1:T(8,128)(2,1)} %get-tuple-element.100, bf16[16,160,1280]{2,1,0:T(8,128)(2,1)} %fusion.26), kind=kOutput, calls=%fused_computation.8.clone.1 | convolution fusion | flops 209715712 | bytes 19668996 | tf_op jit(solution)/shard_map/while/body/eval_jaxpr/noi,qoi->nq/dot_general | solution.py:35
  439.3 6.5 %fusion.26 = bf16[16,160,1280]{2,1,0:T(8,128)(2,1)} fusion(bf16[4,16,64,1280]{3,2,1,0:T(8,128)(2,1)} %get-tuple-element.99, s32[]{:T(128)} %get-tuple-element.90, bf16[4,16,64,160]{3,2,1,0:T(8,128)(2,1)} %get-tuple-element.98), kind=kOutput, calls=%fused_computation.2.clone.1 | convolution fusion | flops 419430400 | bytes 9700352 | tf_op jit(solution)/shard_map/while/body/eval_jaxpr/npo,npi->noi/dot_general | solution.py:31
  445.8 14.3 %fusion.27 = f32[4,16,32]{2,1,0:T(8,128)S(1)} fusion(f32[4,16,32]{2,1,0:T(8,128)S(1)} %get-tuple-element.91, s32[]{:T(128)} %get-tuple-element.90, bf16[32,160,1280]{2,0,1:T(8,128)(2,1)} %get-tuple-element.100, bf16[16,160,1280]{2,1,0:T(8,128)(2,1)} %fusion.26), kind=kOutput, calls=%fused_computation.8.clone.1 | convolution fusion | flops 209715712 | bytes 19668996 | tf_op jit(solution)/shard_map/while/body/eval_jaxpr/noi,qoi->nq/dot_general | solution.py:35
  460.1 24.9 %psum.7 = f32[64,32]{1,0:T(8,128)S(1)} all-reduce(f32[64,32]{1,0:T(8,128)S(1)} %bitcast.43), channel_id=1, replica_groups=mesh['dp'=32,'param'=8] {'param'}, use_global_device_ids=true, to_apply=%region_2.3 | all-reduce | flops 2048 | bytes 16384 | tf_op jit(solution)/shard_map/psum | solution.py:42
  485.0 0.6 constant_dynamic-slice_fusion
  (2 shorter events, 0.0 us)
Async XLA Ops:
  6.5 1.9 copy-start
  6.5 52.1 %all-gather.9.cloned.1.call-start = ((), (), s32[]{:S(2)}) async-start(), calls=%async_computation.2 | async-start | bytes 3686400 | tf_op jit(solution)/shard_map/all_gather | solution.py:18
  11.0 257.8 %all-gather.7.cloned.1.call-start = ((), (), s32[]{:S(2)}) async-start(), calls=%async_computation.1 | async-start | bytes 13516800 | tf_op jit(solution)/shard_map/all_gather | solution.py:23
  62.2 314.7 %all-gather.5.cloned.1.call-start = ((), (), s32[]{:S(2)}) async-start(), calls=%async_computation | async-start | bytes 11796480 | tf_op jit(solution)/shard_map/all_gather | solution.py:13
Sparse Core Ops, SparseCore 0:
  11.1 47.5 all-gather.8
  62.3 206.4 all-gather.6
  270.6 106.3 all-gather.4
where the time goes:
time: 495 us; the launch traced here: 492 us
  waiting for transfers between devices  333 us (67%)
  matrix products  89.2 us (18%)
  local copies, waits for them, and re-layouts  31.5 us (6%)
  blocking collectives  24.9 us (5%)
  between operations  13.1 us (3%)
    all_gather x1, waiting for transfers between devices, per_device(): all_queries = lax.all_gather(preconditioned, 'dp', axis=0, tiled=True)  206 us
    all_gather x1, waiting for transfers between devices, per_device(): all_acts = lax.all_gather(activations, 'param', axis=1, tiled=True)  79.2 us
    dot_general x4, matrix products, score_block(): jnp.einsum('noi,qoi->nq', example_grad, all_queries, preferred_element_ty...  57.2 us
    all_gather x1, waiting for transfers between devices, per_device(): mixed_full = lax.all_gather(mixed_in, 'param', axis=1, tiled=True)  47.6 us
    while x1, local copies, waits for them, and re-layouts, per_device(): lax.map(score_block, (err_blocks, act_blocks))  29 us
    dot_general x4, matrix products, score_block(): jnp.einsum('npo,npi->noi', err_part, act_part, preferred_element_type=jnp...  26 us
    psum x1, blocking collectives, per_device(): totals = lax.psum(partial_scores, 'param')  24.9 us
  transfers between devices with their start and end apart: 3, of which 3 were waited for; matrix products, arithmetic and copies ran while one was open for 6% of the time, Pallas kernels for 0%

commit v1 on v0

v1 whole, which is shorter than its diff:
```python
import math

import jax
import jax.numpy as jnp
from jax import lax
from jax.experimental import pallas as pl
from jax.experimental.pallas import tpu as pltpu
from jax.sharding import PartitionSpec as P

MESH = pl.DeviceIdType.MESH
BF16 = jnp.bfloat16
F32 = jnp.float32
QUADS = 16
UNITS = 10
HALF = 640
WIDE = 4 * HALF


def dot(a, b, dims):
    return lax.dot_general(a, b, (dims, ((), ())), preferred_element_type=F32)


def kernel(
    g_in, iinv_in, oinv_in, a_in, e_in, out,
    g, iv, ob, mstage, mbuf, w, abuf, ebuf, eg, acc, part, rbuf,
    lsem, dsem, msend, mrecv, xsend, xrecv, asend, arecv, fsend, frecv,
):
    dp, pa = lax.axis_index("dp"), lax.axis_index("param")
    zh, x, y = dp // 16, (dp // 4) % 4, dp % 4
    zl, c = pa // 2, pa % 2
    z = zh * 4 + zl
    o = 1 - c
    slot = x * 4 + y

    def at_z(k):
        t = (z + k + 8) % 8
        return ((t // 4) * 16 + slot, (t % 4) * 2 + c)

    def at_xy(dx, dy):
        return (zh * 16 + ((x + dx + 4) % 4) * 4 + (y + dy + 4) % 4, pa)

    partner = (dp, zl * 2 + o)

    def remote(src, dst, ssem, rsem, dev):
        return pltpu.make_async_remote_copy(src, dst, ssem, rsem, device_id=dev, device_id_type=MESH)

    def half_at(ref, h):
        return ref.at[:, :, pl.ds(pl.multiple_of(h * HALF, 128), HALF)]

    loads = [
        pltpu.make_async_copy(g_in, g, lsem.at[0]),
        pltpu.make_async_copy(iinv_in.at[:, pl.ds(pl.multiple_of(o * HALF, 128), HALF)], iv.at[1], lsem.at[1]),
        pltpu.make_async_copy(iinv_in.at[:, pl.ds(pl.multiple_of(c * HALF, 128), HALF)], iv.at[0], lsem.at[2]),
        pltpu.make_async_copy(oinv_in.at[pl.ds(pl.multiple_of(zl * 320, 64), 320)], ob, lsem.at[3]),
        pltpu.make_async_copy(half_at(a_in, c), abuf.at[:, zl, c], lsem.at[4]),
        pltpu.make_async_copy(e_in, ebuf.at[c], lsem.at[5]),
    ]
    for cp in loads:
        cp.start()

    barrier = pltpu.get_barrier_semaphore()
    for dev in (at_z(1), at_z(-1), at_xy(1, 0), at_xy(-1, 0), at_xy(0, 1), at_xy(0, -1)):
        pl.semaphore_signal(barrier, inc=1, device_id=dev, device_id_type=MESH)
    for j in range(1, 8):
        pl.semaphore_signal(barrier, inc=1, device_id=(dp, (pa + j) % 8), device_id_type=MESH)
    pl.semaphore_wait(barrier, 13)

    loads[0].wait()
    loads[1].wait()
    mstage[...] = dot(g[...], iv[1], ((1,), (0,))).astype(BF16)
    swap_m = remote(mstage, mbuf.at[z, c], dsem.at[0], dsem.at[1], partner)
    swap_m.start()
    loads[2].wait()
    mbuf[z, c] = dot(g[...], iv[0], ((1,), (0,))).astype(BF16)

    def m_copy(d, j, i):
        block = (z - d * j + 8) % 8
        which = c if i == 0 else o
        ref = mbuf.at[block, which]
        k = 0 if d > 0 else 1
        return remote(ref, ref, msend.at[k, j, i], mrecv.at[k, j, i], at_z(d))

    sent_m = []
    swap_a = remote(half_at(a_in, o), abuf.at[:, zl, c], dsem.at[2], dsem.at[3], partner)
    swap_e = remote(e_in, ebuf.at[c], dsem.at[4], dsem.at[5], partner)
    for j in range(4):
        for i in range(2):
            if j == 0 and i == 1:
                swap_m.wait_recv()
            for k, d in enumerate((1, -1)):
                if j > 0:
                    m_copy(d, j - 1, i).wait_recv()
                if j < 3 or i == k:
                    cp = m_copy(d, j, i)
                    cp.start()
                    sent_m.append(cp)
        if j == 0:
            swap_a.start()
            swap_e.start()
            for cp in loads[3:]:
                cp.wait()
    swap_a.wait_recv()

    def a_copy(d, j, k):
        block = (zl - d * j + 8) % 4
        ref = abuf.at[k, block]
        i = 0 if d > 0 else 1
        return remote(ref, ref, asend, arecv.at[i, j, k], at_z(d))

    def a_step(j, k):
        for d in (1, -1):
            there = (zl >= j) if d > 0 else (zl <= 3 - j)
            more = (zl < 3) if d > 0 else (zl > 0)

            @pl.when(there & (k >= 0) & (k < QUADS))
            def _():
                if j > 0:
                    a_copy(d, j - 1, k).wait_recv()
                if j < 3:

                    @pl.when(more)
                    def _():
                        a_copy(d, j, k).start()

    a_step(0, jnp.int32(0))
    a_step(0, jnp.int32(1))
    m_copy(1, 3, 0).wait_recv()
    m_copy(-1, 3, 1).wait_recv()

    p0 = dot(ob[...], mbuf[0:4].reshape(1280, HALF), ((1,), (0,))).reshape(40, 8, HALF)
    p1 = dot(ob[...], mbuf[4:8].reshape(1280, HALF), ((1,), (0,))).reshape(40, 8, HALF)
    p = jnp.concatenate([p0, p1], axis=1).astype(BF16).reshape(UNITS, 4, 16, HALF)
    for k in range(4):
        w[:, slot, :, k * HALF : (k + 1) * HALF] = p[:, k]

    def place(first, d1, d2):
        dx, dy = (d1, d2) if first == 0 else (d2, d1)
        return ((x + dx + 4) % 4) * 4 + (y + dy + 4) % 4

    def neighbour(first, axis, d):
        return at_xy(d, 0) if (first == axis) else at_xy(0, d)

    def x_copy(v, first, axis, d, d1, whole):
        u = 2 * v + first
        k = 0 if d > 0 else 1
        if axis == 0:
            s = place(first, 0 if whole else -d, 0)
            sem = k if whole else 2 + k
        else:
            s = place(first, d1, 0 if whole else -d)
            sem = 4 + (d1 + 1) * 4 + (k if whole else 2 + k)
        ref = w.at[u, s]
        if not whole:
            ref = ref.at[:, pl.ds(k * 2 * HALF, 2 * HALF)]
        return remote(ref, ref, xsend.at[u], xrecv.at[u, sem], neighbour(first, axis, d))

    both = (1, -1)

    def stage0(v):
        for d in both:
            for first in (0, 1):
                x_copy(v, first, 0, d, 0, True).start()
        for d in both:
            for first in (0, 1):
                x_copy(v, first, 1, d, 0, True).start()

    def stage1(v):
        for d in both:
            for first in (0, 1):
                x_copy(v, first, 0, d, 0, True).wait_recv()
                x_copy(v, first, 0, d, 0, False).start()
                for e in both:
                    x_copy(v, first, 1, e, -d, True).start()
        for d in both:
            for first in (0, 1):
                x_copy(v, first, 1, d, 0, True).wait_recv()
                x_copy(v, first, 1, d, 0, False).start()

    def stage2(v):
        for first in (0, 1):
            for d in both:
                x_copy(v, first, 0, d, 0, False).wait_recv()
            for e in both:
                x_copy(v, first, 1, e, 2, True).start()
        for d1 in both:
            for d in both:
                for first in (0, 1):
                    x_copy(v, first, 1, d, d1, True).wait_recv()
                    x_copy(v, first, 1, d, d1, False).start()

    def stage3(v):
        for d in both:
            for first in (0, 1):
                x_copy(v, first, 1, d, 2, True).wait_recv()
                x_copy(v, first, 1, d, 2, False).start()

    def stage4(v):
        for d1 in (0, 1, -1, 2):
            for d in both:
                for first in (0, 1):
                    x_copy(v, first, 1, d, d1, False).wait_recv()

    def example_grads(k):
        a4 = abuf[k].astype(F32).reshape(8, 4, 8, HALF)
        for pair in range(2):
            acts = [a4[:, 2 * pair + i].reshape(64, HALF).astype(BF16) for i in range(2)]
            for cc in range(2):
                grads = [
                    dot(ebuf[cc, k * 4 + 2 * pair + i], acts[i], ((0,), (0,))).reshape(20, 8, HALF)
                    for i in range(2)
                ]
                both_images = jnp.concatenate(grads, axis=1).astype(BF16).reshape(5, 4, 16, HALF)
                for j in range(4):
                    eg[5 * cc : 5 * cc + 5, k * 2 + pair, :, j * HALF : (j + 1) * HALF] = both_images[:, j]

    swap_e.wait_recv()

    def step(t, carry):
        v = t // 3

        @pl.when((t % 3 == 0) & (v < 5))
        def _():
            stage0(v)

        a_step(0, t + 2)

        @pl.when((t % 3 == 0) & (v >= 1) & (v <= 5))
        def _():
            stage3(v - 1)

        @pl.when((t % 3 == 1) & (v < 5))
        def _():
            stage1(v)

        @pl.when((t % 3 == 1) & (v >= 1) & (v <= 5))
        def _():
            stage4(v - 1)

        @pl.when((t % 3 == 2) & (v < 5))
        def _():
            stage2(v)

        a_step(1, t)
        a_step(2, t - 1)
        a_step(3, t - 2)

        @pl.when((t >= 2) & (t < QUADS + 2))
        def _():
            example_grads(t - 2)

        return carry

    lax.fori_loop(0, QUADS + 2, step, 0)

    acc[...] = jnp.zeros_like(acc)

    def score(u, carry):
        acc[...] += dot(eg[u].reshape(512, WIDE), w[u].reshape(256, WIDE), ((1,), (1,)))
        return carry

    lax.fori_loop(0, UNITS, score, 0)
    row = lax.broadcasted_iota(jnp.int32, (512, 256), 0)
    col = lax.broadcasted_iota(jnp.int32, (512, 256), 1)
    sums = jnp.where(row % 8 == col % 8, acc[...], 0.0).reshape(64, 8, 256).sum(axis=1)
    col = lax.broadcasted_iota(jnp.int32, (256, 128), 0)
    query = lax.broadcasted_iota(jnp.int32, (256, 128), 1)
    pick = jnp.where(((col // 8) % 2) * 16 + col // 16 == query, 1.0, 0.0).astype(F32)
    part[...] = jnp.dot(sums, pick, preferred_element_type=F32, precision=lax.Precision.HIGHEST)

    shares = []
    for j in range(1, 8):
        to = (pa + j) % 8
        cp = remote(part.at[pl.ds(pl.multiple_of(to * 8, 8), 8)], rbuf.at[j - 1], fsend.at[j - 1], frecv.at[j - 1], (dp, to))
        cp.start()
        shares.append(cp)
    total = part[pl.ds(pl.multiple_of(pa * 8, 8), 8)]
    for j in range(7):
        shares[j].wait_recv()
        total = total + rbuf[j]
    out[...] = total[:, :32] * (1.0 / (1280 * math.sqrt(64)))

    for cp in shares + sent_m + [swap_m, swap_a, swap_e]:
        cp.wait_send()

    def all_sent(u, carry):
        ref = w.at[u, pl.ds(0, 15)]
        remote(ref, ref, xsend.at[u], xrecv.at[u, 0], partner).wait_send()
        return carry

    lax.fori_loop(0, UNITS, all_sent, 0)
    inner = (zl == 1) | (zl == 2)

    @pl.when(inner)
    def _():
        ref = w.at[pl.ds(0, 5)]
        remote(ref, ref, asend, xrecv.at[0, 0], partner).wait_send()

    @pl.when(jnp.logical_not(inner))
    def _():
        ref = w.at[0]
        remote(ref, ref, asend, xrecv.at[0, 0], partner).wait_send()


def per_device(query_grads, in_inverse, out_inverse, activations, errors):
    dma = pltpu.SemaphoreType.DMA
    return pl.pallas_call(
        kernel,
        out_shape=jax.ShapeDtypeStruct((8, 32), F32),
        in_specs=[pl.BlockSpec(memory_space=pl.ANY)] * 5,
        out_specs=pl.BlockSpec(memory_space=pltpu.VMEM),
        scratch_shapes=[
            pltpu.VMEM((160, 1280), BF16),
            pltpu.VMEM((2, 1280, HALF), BF16),
            pltpu.VMEM((320, 1280), BF16),
            pltpu.VMEM((160, HALF), BF16),
            pltpu.VMEM((8, 2, 160, HALF), BF16),
            pltpu.VMEM((UNITS, 16, 16, WIDE), BF16),
            pltpu.VMEM((QUADS, 4, 2, 32, HALF), BF16),
            pltpu.VMEM((2, 64, 64, 160), BF16),
            pltpu.VMEM((UNITS, 32, 16, WIDE), BF16),
            pltpu.VMEM((512, 256), F32),
            pltpu.VMEM((64, 128), F32),
            pltpu.VMEM((7, 8, 128), F32),
            dma((6,)),
            dma((6,)),
            dma((2, 4, 2)),
            dma((2, 4, 2)),
            dma((UNITS,)),
            dma((UNITS, 20)),
            dma,
            dma((2, 3, QUADS)),
            dma((7,)),
            dma((7,)),
        ],
        compiler_params=pltpu.CompilerParams(
            collective_id=0, has_side_effects=True, vmem_limit_bytes=63 * 1024 * 1024
        ),
        cost_estimate=pl.CostEstimate(flops=4 * 10**9, bytes_accessed=10**7, transcendentals=0),
    )(
        query_grads.reshape(160, 1280),
        in_inverse,
        out_inverse,
        activations.reshape(QUADS, 32, 1280),
        errors,
    )


def solution(mesh):
    return jax.shard_map(
        per_device,
        mesh=mesh,
        in_specs=(P("dp", "param", None), P(), P(), P("dp", "param", None), P("dp", None, "param")),
        out_specs=P(("dp", "param"), None),
        check_vma=False,
    )
```

time: 495 us -> 148 us (0.30)
  waiting for transfers between devices: 333 us -> 0 us
  Pallas kernels: 0 us -> 147 us
  matrix products: 89.2 us -> 0 us
  local copies, waits for them, and re-layouts: 31.5 us -> 1.28 us
  blocking collectives: 24.9 us -> 0 us
  between operations: 13.1 us -> 0.01 us
    all_gather x3 -> x0, waiting for transfers between devices: 333 us -> none  [the longest x1 206 us: per_device(): all_queries = lax.all_gather(preconditioned, 'dp', axis=0, tiled=True)]
    pallas_call x0 -> x1, Pallas kernels: none -> 147 us  [per_device(): pl.pallas_call(kernel, out_shape=jax.ShapeDtypeStruct((8, 32), F32), in_s...]
    dot_general x10 -> x0, matrix products: 89.2 us -> none  [the longest x4 57.2 us: score_block(): jnp.einsum('noi,qoi->nq', example_grad, all_queries, preferred_element_ty...]
    while x1 -> x0, local copies, waits for them, and re-layouts: 29 us -> none  [per_device(): lax.map(score_block, (err_blocks, act_blocks))]
    psum x1 -> x0, blocking collectives: 24.9 us -> none  [per_device(): totals = lax.psum(partial_scores, 'param')]
  transfers between devices with their start and end apart: 3 -> 0, of which waited for: 3 -> 0; matrix products, arithmetic and copies ran while one was open for 6% -> 0% of each run, Pallas kernels for 0% -> 0%
where the time goes in v1:
time: 148 us
  Pallas kernels  147 us (99%)
    pallas_call x1, Pallas kernels, per_device(): pl.pallas_call(kernel, out_shape=jax.ShapeDtypeStruct((8, 32), F32), in_s...  147 us

profile of v1, /device:TPU:1, one launch (start us, length us, event | category | flops | bytes accessed | tf_op | source)
XLA Modules:
  0.0 147.8 jit_solution(4579050224861298484)
XLA Ops:
  0.0 146.5 %shard_map.55 = f32[8,32]{1,0:T(8,128)} custom-call(bf16[160,1280]{1,0:T(8,128)(2,1)} %bitcast.3, bf16[1280,1280]{1,0:T(8,128)(2,1)} %iinv_in.1, bf16[1280,1280]{1,0:T(8,128)(2,1)} %oinv_in.1, bf16[16,32,1280]{2,1,0:T(8,128)(2,1)} %bitcast.2, bf16[64,64,160]{2,1,0:T(8,128)(2,1)} %e_in.1), custom_call_target="tpu_custom_call" | custom-call | flops 4000000000 | bytes 10000000 | tf_op jit(solution)/shard_map/pallas_call | solution.py:306
  146.6 1.3 copy.7

commit v2 on v1

v2 whole, which is shorter than its diff:
```python
import math

import jax
import jax.numpy as jnp
from jax import lax
from jax.experimental import pallas as pl
from jax.experimental.pallas import tpu as pltpu
from jax.sharding import PartitionSpec as P

MESH = pl.DeviceIdType.MESH
BF16 = jnp.bfloat16
F32 = jnp.float32
GROUPS = 8
AHEAD = 2
LAG = 3
LAST = 24
UNITS = 10
HALF = 640
WIDE = 20 * 128
CUTS = ((0, 384), (384, 640))
EARLY = 384


def dot(a, b, dims):
    return lax.dot_general(a, b, (dims, ((), ())), preferred_element_type=F32)


def kernel(
    g_in, iinv_in, oinv_in, a_in, e_in, out,
    g, iv, ob, mstage0, mstage1, mbuf0, mbuf1, w, abuf, ebuf, et, eg, acc, part, rbuf,
    lsem, msend, mrecv, mdsend, mdrecv, esend, erecv, xsend, xrecv, asend, arecv, adsend, adrecv, fsend, frecv,
):
    dp, pa = lax.axis_index("dp"), lax.axis_index("param")
    zh, x, y = dp // 16, (dp // 4) % 4, dp % 4
    zl, c = pa // 2, pa % 2
    z = zh * 4 + zl
    h = zl % 2
    near = zl + 1 - 2 * h
    slot = x * 4 + y

    def at_z(k):
        t = (z + k + 8) % 8
        return ((t // 4) * 16 + slot, (t % 4) * 2 + c)

    def at_xy(dx, dy):
        return (zh * 16 + ((x + dx + 4) % 4) * 4 + (y + dy + 4) % 4, pa)

    partner = (dp, zl * 2 + 1 - c)

    def remote(src, dst, ssem, rsem, dev):
        return pltpu.make_async_remote_copy(src, dst, ssem, rsem, device_id=dev, device_id_type=MESH)

    def lanes(half):
        return pl.ds(pl.multiple_of(half * HALF, 128), HALF)

    loads = [
        pltpu.make_async_copy(g_in, g, lsem.at[0]),
        pltpu.make_async_copy(iinv_in.at[:, lanes(1 - h)], iv.at[1], lsem.at[1]),
        pltpu.make_async_copy(iinv_in.at[:, lanes(h)], iv.at[0], lsem.at[2]),
        pltpu.make_async_copy(e_in, ebuf, lsem.at[3]),
        pltpu.make_async_copy(a_in.at[:, :, :, lanes(h)], abuf.at[:, zl, c], lsem.at[4]),
    ] + [
        pltpu.make_async_copy(
            oinv_in.at[pl.ds(pl.multiple_of((zl - h + k) * 320 + c * 160, 32), 160)], ob.at[pl.ds(k * 160, 160)], lsem.at[5 + k]
        )
        for k in (0, 1)
    ]
    for cp in loads:
        cp.start()

    barrier = pltpu.get_barrier_semaphore()
    for dev in (at_z(1), at_z(-1), at_z(2), at_z(-2), at_xy(1, 0), at_xy(-1, 0), at_xy(0, 1), at_xy(0, -1)):
        pl.semaphore_signal(barrier, inc=1, device_id=dev, device_id_type=MESH)
    for j in range(1, 8):
        pl.semaphore_signal(barrier, inc=1, device_id=(dp, (pa + j) % 8), device_id_type=MESH)
    pl.semaphore_wait(barrier, 15)

    mstage, mbuf = (mstage0, mstage1), (mbuf0, mbuf1)

    def m_copy(n, d, kind):
        k = (0 if d > 0 else 4) + kind
        if kind == 0:
            return remote(mstage[n], mbuf[n].at[z, c], msend.at[n, k], mrecv.at[n, k], at_z(d))
        ref = mbuf[n].at[(z - d * (kind - 1) + 8) % 8, c]
        if kind == 3:
            ref = ref.at[pl.ds(0 if d > 0 else 80, 80)]
        return remote(ref, ref, msend.at[n, k], mrecv.at[n, k], at_z(2 * d))

    def m_share(n, j, k):
        ref = mbuf[n].at[(z + j + 8) % 8, c]
        return remote(ref, ref, mdsend.at[n, k], mdrecv.at[n, k], partner)

    both = (1, -1)
    sent = []

    def send(cp):
        cp.start()
        sent.append(cp)

    def m_other(n):
        lo, hi = CUTS[n]
        mstage[n][...] = dot(g[...], iv[1, :, lo:hi], ((1,), (0,))).astype(BF16)

    def m_own(n):
        lo, hi = CUTS[n]
        mbuf[n][z, c] = dot(g[...], iv[0, :, lo:hi], ((1,), (0,))).astype(BF16)

    def m_first(n):
        for i, d in enumerate(both):
            m_copy(n, d, 0).wait_recv()
            send(m_copy(n, d, 2))
            send(m_share(n, -d, 1 + i))

    def m_second(n):
        for i, d in enumerate(both):
            m_copy(n, d, 1).wait_recv()
            send(m_copy(n, d, 3))
            send(m_share(n, -2 * d, 3 + i))

    def m_last(n):
        for i, d in enumerate(both):
            m_copy(n, d, 2).wait_recv()
            send(m_share(n, -3 * d, 5 + i))
        for d in both:
            m_copy(n, d, 3).wait_recv()
        send(m_share(n, 4, 7))
        for k, j in enumerate((0, -1, 1, -2, 2, -3, 3, 4)):
            m_share(n, j, k).wait_recv()

    def turn(i, carry):
        et[h, i] = ebuf[pl.ds(2 * i, 2)].reshape(128, 160).T
        return carry

    loads[0].wait()
    loads[1].wait()
    m_other(0)
    for d in both:
        send(m_copy(0, d, 0))
    loads[2].wait()
    m_own(0)
    for d in both:
        send(m_copy(0, d, 1))
    send(m_share(0, 0, 0))
    m_other(1)
    m_own(1)
    m_first(0)
    m_second(0)
    for kind in (0, 1):
        for d in both:
            send(m_copy(1, d, kind))
    send(m_share(1, 0, 0))
    loads[3].wait()
    lax.fori_loop(0, 32, turn, 0)
    loads[4].wait()

    def e_copy(k):
        ref = et.at[h, pl.ds(k * 4, 4)]
        return remote(ref, ref, esend, erecv.at[k], (dp, near * 2 + c))

    def a_send(k):
        @pl.when(k < GROUPS)
        def _():
            e_copy(k).start()
            for d in both:

                @pl.when((zl + d >= 0) & (zl + d <= 3))
                def _():
                    a_copy(k, zl, a_in.at[k, :, :, lanes(1 - h)], d).start()

            for d in both:

                @pl.when((zl + 2 * d >= 0) & (zl + 2 * d <= 3))
                def _():
                    a_copy(k, zl, abuf.at[k, zl, c], 2 * d).start()

    def a_copy(k, block, src, d):
        return remote(src, abuf.at[k, block, c], asend, arecv.at[block, k], at_z(d))

    def a_share(k, block):
        ref = abuf.at[k, block, c]
        return remote(ref, ref, adsend, adrecv.at[block, k], partner)

    def middle(block):
        return ((zl == 1) & (block == 0)) | ((zl == 2) & (block == 3))

    def a_pass(k):
        for block in (0, 3):

            @pl.when(middle(block))
            def _():
                ref = abuf.at[k, block, c]
                a_copy(k, block, ref, 1).wait_recv()
                a_copy(k, block, ref, 2 if block == 0 else -2).start()
                a_share(k, block).start()

    def a_collect(k):
        for j in range(1, 4):
            block = (zl + j) % 4

            @pl.when(jnp.logical_not(middle(block)))
            def _():
                a_copy(k, block, abuf.at[k, block, c], 1).wait_recv()
                a_share(k, block).start()

    def a_ready(k):
        for j in range(4):
            a_share(k, (zl + j) % 4).wait_recv()
        e_copy(k).wait_recv()

    def place(first, d1, d2):
        dx, dy = (d1, d2) if first == 0 else (d2, d1)
        return ((x + dx + 4) % 4) * 4 + (y + dy + 4) % 4

    def neighbour(first, axis, d):
        return at_xy(d, 0) if (first == axis) else at_xy(0, d)

    def x_copy(v, first, axis, d, d1, whole):
        u = 2 * v + first
        k = 0 if d > 0 else 1
        if axis == 0:
            s = place(first, 0 if whole else -d, 0)
            sem = k if whole else 2 + k
        else:
            s = place(first, d1, 0 if whole else -d)
            sem = 4 + (d1 + 1) * 4 + (k if whole else 2 + k)
        ref = w.at[u, s]
        if not whole:
            ref = ref.at[:, pl.ds(k * 2 * HALF, 2 * HALF)]
        return remote(ref, ref, xsend.at[u], xrecv.at[u, sem], neighbour(first, axis, d))

    def stage0(v):
        for d in both:
            for first in (0, 1):
                x_copy(v, first, 0, d, 0, True).start()
        for d in both:
            for first in (0, 1):
                x_copy(v, first, 1, d, 0, True).start()

    def stage1(v):
        for d in both:
            for first in (0, 1):
                x_copy(v, first, 0, d, 0, True).wait_recv()
                x_copy(v, first, 0, d, 0, False).start()
                for e in both:
                    x_copy(v, first, 1, e, -d, True).start()
        for d in both:
            for first in (0, 1):
                x_copy(v, first, 1, d, 0, True).wait_recv()
                x_copy(v, first, 1, d, 0, False).start()

    def stage2(v):
        for first in (0, 1):
            for d in both:
                x_copy(v, first, 0, d, 0, False).wait_recv()
            for e in both:
                x_copy(v, first, 1, e, 2, True).start()
        for d1 in both:
            for d in both:
                for first in (0, 1):
                    x_copy(v, first, 1, d, d1, True).wait_recv()
                    x_copy(v, first, 1, d, d1, False).start()

    def stage3(v):
        for d in both:
            for first in (0, 1):
                x_copy(v, first, 1, d, 2, True).wait_recv()
                x_copy(v, first, 1, d, 2, False).start()

    def stage4(v):
        for d1 in (0, 1, -1, 2):
            for d in both:
                for first in (0, 1):
                    x_copy(v, first, 1, d, d1, False).wait_recv()

    def precondition(n):
        lo, hi = CUTS[n]
        p = [
            dot(ob[...], mbuf[n][4 * k : 4 * k + 4].reshape(1280, hi - lo), ((1,), (0,))).reshape(40, 8, hi - lo)
            for k in (0, 1)
        ]
        p = jnp.concatenate(p, axis=1).astype(BF16)
        for i in range(lo // 128, hi // 128):
            for k in range(40):
                u, place_in = 2 * i + k // 20, 128 * (k % 20)
                w[u, slot, :, place_in : place_in + 128] = p[k, :, 128 * i - lo : 128 * i - lo + 128]

    for k in range(GROUPS):
        a_share(k, zl).start()
    loads[5].wait()
    loads[6].wait()
    m_last(0)
    precondition(0)
    for v in range(3):
        stage0(v)
    m_first(1)
    m_second(1)
    a_send(jnp.int32(0))
    stage1(0)
    m_last(1)
    for k in range(1, AHEAD):
        a_send(jnp.int32(k))
    precondition(1)
    acc[...] = jnp.zeros_like(acc)

    left_half = lax.broadcasted_iota(jnp.int32, (160, 128), 1) < 64

    def example_grads(k):
        a8 = abuf[k].astype(F32).reshape(8, 2, 4, 8, HALF)
        for pair in range(4):
            quad, i = pair // 2, 2 * (pair % 2)
            acts = jnp.concatenate([a8[:, quad, i].reshape(64, HALF), a8[:, quad, i + 1].reshape(64, HALF)], axis=0).astype(BF16)
            for cc in range(2):
                errs = et[cc, k * 4 + pair].astype(F32)
                pieces = [
                    dot(jnp.where(left_half, errs, 0.0).astype(BF16), acts, ((1,), (0,))).reshape(20, 8, HALF),
                    dot(jnp.where(left_half, 0.0, errs).astype(BF16), acts, ((1,), (0,))).reshape(20, 8, HALF),
                ]
                both_images = jnp.concatenate(pieces, axis=1).astype(BF16)
                for i in range(5):
                    for j in range(20):
                        eg[2 * i + cc, k * 4 + pair, :, j * 128 : j * 128 + 128] = both_images[j, :, i * 128 : i * 128 + 128]

    def score(v, lo, hi):
        total = acc[lo:hi]
        for u in (2 * v, 2 * v + 1):
            total += dot(eg[u, lo // 16 : hi // 16].reshape(hi - lo, WIDE), w[u].reshape(256, WIDE), ((1,), (1,)))
        acc[lo:hi] = total

    def step(t, carry):
        v = t // 3

        @pl.when((t % 3 == 0) & (v >= 1) & (v < 5))
        def _():
            stage1(v)

        @pl.when((t % 3 == 0) & (v < 2))
        def _():
            stage0(v + 3)

        @pl.when((t % 3 == 1) & (v >= 1) & (v <= 5))
        def _():
            stage2(v - 1)

        @pl.when((t % 3 == 2) & (v >= 2) & (v <= 6))
        def _():
            stage3(v - 2)

        k = t // 2

        @pl.when((t % 2 == 0) & (k < GROUPS))
        def _():
            a_pass(k)
            a_send(k + AHEAD)

        @pl.when((t % 2 == 1) & (k >= LAG) & (k < GROUPS + LAG))
        def _():
            a_collect(k - LAG)

        @pl.when((t % 2 == 0) & (k >= LAG + 1) & (k < GROUPS + LAG + 1))
        def _():
            a_ready(k - LAG - 1)
            example_grads(k - LAG - 1)

        @pl.when((t % 3 == 2) & (v >= 3) & (v <= 7))
        def _():
            stage4(v - 3)

        @pl.when((t >= LAST - 5) & (t < LAST))
        def _():
            score(t - LAST + 5, 0, EARLY)

        return carry

    lax.fori_loop(0, LAST, step, 0)

    def score_late(v, carry):
        score(v, EARLY, 512)
        return carry

    lax.fori_loop(0, 5, score_late, 0)

    row = lax.broadcasted_iota(jnp.int32, (512, 256), 0)
    col = lax.broadcasted_iota(jnp.int32, (512, 256), 1)
    sums = jnp.where(row % 8 == col % 8, acc[...], 0.0).reshape(64, 8, 256).sum(axis=1)
    col = lax.broadcasted_iota(jnp.int32, (256, 128), 0)
    query = lax.broadcasted_iota(jnp.int32, (256, 128), 1)
    pick = jnp.where(((col // 8) % 2) * 16 + col // 16 == query, 1.0, 0.0).astype(F32)
    part[...] = jnp.dot(sums, pick, preferred_element_type=F32, precision=lax.Precision.HIGHEST)

    shares = []
    for j in range(1, 8):
        to = (pa + j) % 8
        cp = remote(part.at[pl.ds(pl.multiple_of(to * 8, 8), 8)], rbuf.at[j - 1], fsend.at[j - 1], frecv.at[j - 1], (dp, to))
        cp.start()
        shares.append(cp)
    total = part[pl.ds(pl.multiple_of(pa * 8, 8), 8)]
    for j in range(7):
        shares[j].wait_recv()
        total = total + rbuf[j]
    out[...] = total[:, :32] * (1.0 / (1280 * math.sqrt(64)))

    for cp in shares + sent:
        cp.wait_send()

    def all_sent(u, carry):
        ref = w.at[u, pl.ds(0, 15)]
        remote(ref, ref, xsend.at[u], xrecv.at[u, 0], partner).wait_send()
        return carry

    lax.fori_loop(0, UNITS, all_sent, 0)
    remote(et.at[0], et.at[0], esend, erecv.at[0], partner).wait_send()
    ref = abuf.at[:, :, 0]
    remote(ref, ref, adsend, arecv.at[0, 0], partner).wait_send()
    inner = (zl == 1) | (zl == 2)

    @pl.when(inner)
    def _():
        ref = abuf.at[:, :, 0]
        remote(ref, ref, asend, arecv.at[0, 0], partner).wait_send()

    @pl.when(jnp.logical_not(inner))
    def _():
        ref = abuf.at[:, pl.ds(0, 2), 0]
        remote(ref, ref, asend, arecv.at[0, 0], partner).wait_send()


def per_device(query_grads, in_inverse, out_inverse, activations, errors):
    dma = pltpu.SemaphoreType.DMA
    return pl.pallas_call(
        kernel,
        out_shape=jax.ShapeDtypeStruct((8, 32), F32),
        in_specs=[pl.BlockSpec(memory_space=pl.ANY)] * 5,
        out_specs=pl.BlockSpec(memory_space=pltpu.VMEM),
        scratch_shapes=[
            pltpu.VMEM((160, 1280), BF16),
            pltpu.VMEM((2, 1280, HALF), BF16),
            pltpu.VMEM((320, 1280), BF16),
            pltpu.VMEM((160, 384), BF16),
            pltpu.VMEM((160, 256), BF16),
            pltpu.VMEM((8, 2, 160, 384), BF16),
            pltpu.VMEM((8, 2, 160, 256), BF16),
            pltpu.VMEM((UNITS, 16, 16, WIDE), BF16),
            pltpu.VMEM((GROUPS, 4, 2, 2, 32, HALF), BF16),
            pltpu.VMEM((64, 64, 160), BF16),
            pltpu.VMEM((2, 32, 160, 128), BF16),
            pltpu.VMEM((UNITS, 32, 16, WIDE), BF16),
            pltpu.VMEM((512, 256), F32),
            pltpu.VMEM((64, 128), F32),
            pltpu.VMEM((7, 8, 128), F32),
            dma((7,)),
            dma((2, 8)),
            dma((2, 8)),
            dma((2, 8)),
            dma((2, 8)),
            dma,
            dma((GROUPS,)),
            dma((UNITS,)),
            dma((UNITS, 20)),
            dma,
            dma((4, GROUPS)),
            dma,
            dma((4, GROUPS)),
            dma((7,)),
            dma((7,)),
        ],
        compiler_params=pltpu.CompilerParams(
            collective_id=0, has_side_effects=True, vmem_limit_bytes=63 * 1024 * 1024
        ),
        cost_estimate=pl.CostEstimate(flops=4 * 10**9, bytes_accessed=10**7, transcendentals=0),
    )(
        query_grads.reshape(160, 1280),
        in_inverse,
        out_inverse,
        activations.reshape(GROUPS, 2, 32, 1280),
        errors,
    )


def solution(mesh):
    return jax.shard_map(
        per_device,
        mesh=mesh,
        in_specs=(P("dp", "param", None), P(), P(), P("dp", "param", None), P("dp", None, "param")),
        out_specs=P(("dp", "param"), None),
        check_vma=False,
    )
```

time: 148 us -> 126 us (0.85)
  Pallas kernels: 147 us -> 125 us
    pallas_call x1, Pallas kernels: 147 us -> 125 us  [per_device(): pl.pallas_call(kernel, out_shape=jax.ShapeDtypeStruct((8, 32), F32), in_s...]
where the time goes in v2:
time: 126 us
  Pallas kernels  125 us (99%)
  local copies, waits for them, and re-layouts  1.28 us (1%)
    pallas_call x1, Pallas kernels, per_device(): pl.pallas_call(kernel, out_shape=jax.ShapeDtypeStruct((8, 32), F32), in_s...  125 us

profile of v2, /device:TPU:1, one launch (start us, length us, event | category | flops | bytes accessed | tf_op | source)
XLA Modules:
  0.0 126.1 jit_solution(7150020623214430546)
XLA Ops:
  0.0 124.8 %shard_map.55 = f32[8,32]{1,0:T(8,128)} custom-call(bf16[160,1280]{1,0:T(8,128)(2,1)} %bitcast.3, bf16[1280,1280]{1,0:T(8,128)(2,1)} %iinv_in.1, bf16[1280,1280]{1,0:T(8,128)(2,1)} %oinv_in.1, bf16[8,2,32,1280]{3,2,1,0:T(8,128)(2,1)} %bitcast.2, bf16[64,64,160]{2,1,0:T(8,128)(2,1)} %e_in.1), custom_call_target="tpu_custom_call" | custom-call | flops 4000000000 | bytes 10000000 | tf_op jit(solution)/shard_map/pallas_call | solution.py:429
  124.8 1.3 %copy.7 = f32[8,32]{1,0:T(8,128)} copy(f32[8,32]{1,0:T(8,128)} %shard_map.55) | data formatting | bytes 2048

commit v3 on v2

--- a/solution.py
+++ b/solution.py
@@ -11,14 +11,12 @@
 BF16 = jnp.bfloat16
 F32 = jnp.float32
 GROUPS = 8
-AHEAD = 2
-LAG = 3
-LAST = 24
+STEPS = 27
+LATE = 256
 UNITS = 10
 HALF = 640
 WIDE = 20 * 128
-CUTS = ((0, 384), (384, 640))
-EARLY = 384
+CUTS = ((0, 128), (128, 384), (384, 640))
 
 
 def dot(a, b, dims):
@@ -27,7 +25,7 @@
 
 def kernel(
     g_in, iinv_in, oinv_in, a_in, e_in, out,
-    g, iv, ob, mstage0, mstage1, mbuf0, mbuf1, w, abuf, ebuf, et, eg, acc, part, rbuf,
+    g, iv, ob, mstage0, mstage1, mstage2, mbuf0, mbuf1, mbuf2, w, abuf, ebuf, et, eg, acc, part, rbuf,
     lsem, msend, mrecv, mdsend, mdrecv, esend, erecv, xsend, xrecv, asend, arecv, adsend, adrecv, fsend, frecv,
 ):
     dp, pa = lax.axis_index("dp"), lax.axis_index("param")
@@ -75,7 +73,66 @@
         pl.semaphore_signal(barrier, inc=1, device_id=(dp, (pa + j) % 8), device_id_type=MESH)
     pl.semaphore_wait(barrier, 15)
 
-    mstage, mbuf = (mstage0, mstage1), (mbuf0, mbuf1)
+    both = (1, -1)
+
+    def e_copy(k):
+        ref = et.at[h, pl.ds(k * 4, 4)]
+        return remote(ref, ref, esend, erecv.at[k], (dp, near * 2 + c))
+
+    def a_near(k):
+        for d in both:
+
+            @pl.when((zl + d >= 0) & (zl + d <= 3))
+            def _():
+                a_copy(k, zl, a_in.at[k, :, :, lanes(1 - h)], d).start()
+
+    def a_send(k, near=True):
+        @pl.when(k < GROUPS)
+        def _():
+            e_copy(k).start()
+            if near:
+                a_near(k)
+            for d in both:
+
+                @pl.when((zl + 2 * d >= 0) & (zl + 2 * d <= 3))
+                def _():
+                    a_copy(k, zl, abuf.at[k, zl, c], 2 * d).start()
+
+    def a_copy(k, block, src, d):
+        return remote(src, abuf.at[k, block, c], asend, arecv.at[block, k], at_z(d))
+
+    def a_share(k, block):
+        ref = abuf.at[k, block, c]
+        return remote(ref, ref, adsend, adrecv.at[block, k], partner)
+
+    def middle(block):
+        return ((zl == 1) & (block == 0)) | ((zl == 2) & (block == 3))
+
+    def a_pass(k):
+        for block in (0, 3):
+
+            @pl.when(middle(block))
+            def _():
+                ref = abuf.at[k, block, c]
+                a_copy(k, block, ref, 1).wait_recv()
+                a_copy(k, block, ref, 2 if block == 0 else -2).start()
+                a_share(k, block).start()
+
+    def a_collect(k):
+        for j in range(1, 4):
+            block = (zl + j) % 4
+
+            @pl.when(jnp.logical_not(middle(block)))
+            def _():
+                a_copy(k, block, abuf.at[k, block, c], 1).wait_recv()
+                a_share(k, block).start()
+
+    def a_ready(k):
+        for j in range(4):
+            a_share(k, (zl + j) % 4).wait_recv()
+        e_copy(k).wait_recv()
+
+    mstage, mbuf = (mstage0, mstage1, mstage2), (mbuf0, mbuf1, mbuf2)
 
     def m_copy(n, d, kind):
         k = (0 if d > 0 else 4) + kind
@@ -90,7 +147,6 @@
         ref = mbuf[n].at[(z + j + 8) % 8, c]
         return remote(ref, ref, mdsend.at[n, k], mdrecv.at[n, k], partner)
 
-    both = (1, -1)
     sent = []
 
     def send(cp):
@@ -131,81 +187,28 @@
         et[h, i] = ebuf[pl.ds(2 * i, 2)].reshape(128, 160).T
         return carry
 
+    def m_start(n):
+        for kind in (0, 1):
+            for d in both:
+                send(m_copy(n, d, kind))
+        send(m_share(n, 0, 0))
+
+    a_near(0)
     loads[0].wait()
     loads[1].wait()
     m_other(0)
-    for d in both:
-        send(m_copy(0, d, 0))
     loads[2].wait()
     m_own(0)
-    for d in both:
-        send(m_copy(0, d, 1))
-    send(m_share(0, 0, 0))
-    m_other(1)
-    m_own(1)
+    m_start(0)
+    a_near(1)
+    for n in (1, 2):
+        m_other(n)
+        m_own(n)
     m_first(0)
     m_second(0)
-    for kind in (0, 1):
-        for d in both:
-            send(m_copy(1, d, kind))
-    send(m_share(1, 0, 0))
-    loads[3].wait()
-    lax.fori_loop(0, 32, turn, 0)
-    loads[4].wait()
-
-    def e_copy(k):
-        ref = et.at[h, pl.ds(k * 4, 4)]
-        return remote(ref, ref, esend, erecv.at[k], (dp, near * 2 + c))
-
-    def a_send(k):
-        @pl.when(k < GROUPS)
-        def _():
-            e_copy(k).start()
-            for d in both:
-
-                @pl.when((zl + d >= 0) & (zl + d <= 3))
-                def _():
-                    a_copy(k, zl, a_in.at[k, :, :, lanes(1 - h)], d).start()
-
-            for d in both:
-
-                @pl.when((zl + 2 * d >= 0) & (zl + 2 * d <= 3))
-                def _():
-                    a_copy(k, zl, abuf.at[k, zl, c], 2 * d).start()
-
-    def a_copy(k, block, src, d):
-        return remote(src, abuf.at[k, block, c], asend, arecv.at[block, k], at_z(d))
-
-    def a_share(k, block):
-        ref = abuf.at[k, block, c]
-        return remote(ref, ref, adsend, adrecv.at[block, k], partner)
-
-    def middle(block):
-        return ((zl == 1) & (block == 0)) | ((zl == 2) & (block == 3))
-
-    def a_pass(k):
-        for block in (0, 3):
-
-            @pl.when(middle(block))
-            def _():
-                ref = abuf.at[k, block, c]
-                a_copy(k, block, ref, 1).wait_recv()
-                a_copy(k, block, ref, 2 if block == 0 else -2).start()
-                a_share(k, block).start()
-
-    def a_collect(k):
-        for j in range(1, 4):
-            block = (zl + j) % 4
-
-            @pl.when(jnp.logical_not(middle(block)))
-            def _():
-                a_copy(k, block, abuf.at[k, block, c], 1).wait_recv()
-                a_share(k, block).start()
-
-    def a_ready(k):
-        for j in range(4):
-            a_share(k, (zl + j) % 4).wait_recv()
-        e_copy(k).wait_recv()
+    m_start(1)
+    loads[5].wait()
+    loads[6].wait()
 
     def place(first, d1, d2):
         dx, dy = (d1, d2) if first == 0 else (d2, d1)
@@ -284,22 +287,29 @@
                 u, place_in = 2 * i + k // 20, 128 * (k % 20)
                 w[u, slot, :, place_in : place_in + 128] = p[k, :, 128 * i - lo : 128 * i - lo + 128]
 
+    m_last(0)
+    precondition(0)
+    stage0(0)
+    m_first(1)
+    m_second(1)
+    m_start(2)
+    loads[3].wait()
+    loads[4].wait()
+    lax.fori_loop(0, 16, turn, 0)
+    m_last(1)
+    precondition(1)
+    stage0(1)
+    stage0(2)
+    m_first(2)
+    m_second(2)
+    stage1(0)
     for k in range(GROUPS):
         a_share(k, zl).start()
-    loads[5].wait()
-    loads[6].wait()
-    m_last(0)
-    precondition(0)
-    for v in range(3):
-        stage0(v)
-    m_first(1)
-    m_second(1)
-    a_send(jnp.int32(0))
-    stage1(0)
-    m_last(1)
-    for k in range(1, AHEAD):
-        a_send(jnp.int32(k))
-    precondition(1)
+    lax.fori_loop(16, 32, turn, 0)
+    a_send(jnp.int32(0), False)
+    m_last(2)
+    a_send(jnp.int32(1), False)
+    precondition(2)
     acc[...] = jnp.zeros_like(acc)
 
     left_half = lax.broadcasted_iota(jnp.int32, (160, 128), 1) < 64
@@ -326,58 +336,83 @@
             total += dot(eg[u, lo // 16 : hi // 16].reshape(hi - lo, WIDE), w[u].reshape(256, WIDE), ((1,), (1,)))
         acc[lo:hi] = total
 
+    def pick(t, times):
+        on, index = t == times[0], 0
+        for k in range(1, len(times)):
+            on = on | (t == times[k])
+            index = index + jnp.where(t >= times[k], 1, 0)
+        return on, index
+
+    def score_rest(v, carry):
+        score(v, LATE, 512)
+        return carry
+
     def step(t, carry):
-        v = t // 3
-
-        @pl.when((t % 3 == 0) & (v >= 1) & (v < 5))
-        def _():
-            stage1(v)
-
-        @pl.when((t % 3 == 0) & (v < 2))
-        def _():
-            stage0(v + 3)
-
-        @pl.when((t % 3 == 1) & (v >= 1) & (v <= 5))
-        def _():
-            stage2(v - 1)
-
-        @pl.when((t % 3 == 2) & (v >= 2) & (v <= 6))
-        def _():
-            stage3(v - 2)
-
-        k = t // 2
-
-        @pl.when((t % 2 == 0) & (k < GROUPS))
-        def _():
-            a_pass(k)
-            a_send(k + AHEAD)
-
-        @pl.when((t % 2 == 1) & (k >= LAG) & (k < GROUPS + LAG))
-        def _():
-            a_collect(k - LAG)
-
-        @pl.when((t % 2 == 0) & (k >= LAG + 1) & (k < GROUPS + LAG + 1))
-        def _():
-            a_ready(k - LAG - 1)
-            example_grads(k - LAG - 1)
-
-        @pl.when((t % 3 == 2) & (v >= 3) & (v <= 7))
-        def _():
-            stage4(v - 3)
-
-        @pl.when((t >= LAST - 5) & (t < LAST))
-        def _():
-            score(t - LAST + 5, 0, EARLY)
+        on, i = pick(t, (2, 4, 7, 9, 12, 14, 17, 19))
+
+        @pl.when(on)
+        def _(i=i + 0):
+            a_pass(i)
+
+        on, i = pick(t, (2, 4, 7, 9, 12, 14))
+
+        @pl.when(on)
+        def _(i=i + 2):
+            a_send(i)
+
+        on, i = pick(t, (3, 6, 9, 12))
+
+        @pl.when(on)
+        def _(i=i + 1):
+            stage1(i)
+
+        on, i = pick(t, (0, 3))
+
+        @pl.when(on)
+        def _(i=i + 3):
+            stage0(i)
+
+        on, i = pick(t, (4, 7, 10, 13, 16))
+
+        @pl.when(on)
+        def _(i=i + 0):
+            stage2(i)
+
+        on, i = pick(t, (8, 11, 14, 17, 18))
+
+        @pl.when(on)
+        def _(i=i + 0):
+            stage3(i)
+
+        on, i = pick(t, (11, 14, 17, 18, 19))
+
+        @pl.when(on)
+        def _(i=i + 0):
+            stage4(i)
+
+        on, i = pick(t, (8, 10, 13, 15, 18, 20, 23, 25))
+
+        @pl.when(on)
+        def _(i=i + 0):
+            a_collect(i)
+
+        on, i = pick(t, (9, 11, 14, 16, 19, 21, 24, 26))
+
+        @pl.when(on)
+        def _(i=i + 0):
+            a_ready(i)
+            example_grads(i)
+
+        on, i = pick(t, (16, 17, 18, 19, 20))
+
+        @pl.when(on)
+        def _(i=i + 0):
+            score(i, 0, LATE)
 
         return carry
 
-    lax.fori_loop(0, LAST, step, 0)
-
-    def score_late(v, carry):
-        score(v, EARLY, 512)
-        return carry
-
-    lax.fori_loop(0, 5, score_late, 0)
+    lax.fori_loop(0, STEPS, step, 0)
+    lax.fori_loop(0, 5, score_rest, 0)
 
     row = lax.broadcasted_iota(jnp.int32, (512, 256), 0)
     col = lax.broadcasted_iota(jnp.int32, (512, 256), 1)
@@ -435,9 +470,11 @@
             pltpu.VMEM((160, 1280), BF16),
             pltpu.VMEM((2, 1280, HALF), BF16),
             pltpu.VMEM((320, 1280), BF16),
-            pltpu.VMEM((160, 384), BF16),
+            pltpu.VMEM((160, 128), BF16),
             pltpu.VMEM((160, 256), BF16),
-            pltpu.VMEM((8, 2, 160, 384), BF16),
+            pltpu.VMEM((160, 256), BF16),
+            pltpu.VMEM((8, 2, 160, 128), BF16),
+            pltpu.VMEM((8, 2, 160, 256), BF16),
             pltpu.VMEM((8, 2, 160, 256), BF16),
             pltpu.VMEM((UNITS, 16, 16, WIDE), BF16),
             pltpu.VMEM((GROUPS, 4, 2, 2, 32, HALF), BF16),
@@ -448,10 +485,10 @@
             pltpu.VMEM((64, 128), F32),
             pltpu.VMEM((7, 8, 128), F32),
             dma((7,)),
-            dma((2, 8)),
-            dma((2, 8)),
-            dma((2, 8)),
-            dma((2, 8)),
+            dma((3, 8)),
+            dma((3, 8)),
+            dma((3, 8)),
+            dma((3, 8)),
             dma,
             dma((GROUPS,)),
             dma((UNITS,)),

time: 126 us -> 123 us (0.976)
  Pallas kernels: 125 us -> 121 us
    pallas_call x1, Pallas kernels: 125 us -> 121 us  [per_device(): pl.pallas_call(kernel, out_shape=jax.ShapeDtypeStruct((8, 32), F32), in_s...]
where the time goes in v3:
time: 123 us
  Pallas kernels  121 us (98%)
  local copies, waits for them, and re-layouts  1.28 us (1%)
    pallas_call x1, Pallas kernels, per_device(): pl.pallas_call(kernel, out_shape=jax.ShapeDtypeStruct((8, 32), F32), in_s...  121 us

profile of v3, /device:TPU:1, one launch (start us, length us, event | category | flops | bytes accessed | tf_op | source)
XLA Modules:
  0.0 122.7 jit_solution(9675227948128714724)
XLA Ops:
  0.0 121.4 %shard_map.55 = f32[8,32]{1,0:T(8,128)} custom-call(bf16[160,1280]{1,0:T(8,128)(2,1)} %bitcast.3, bf16[1280,1280]{1,0:T(8,128)(2,1)} %iinv_in.1, bf16[1280,1280]{1,0:T(8,128)(2,1)} %oinv_in.1, bf16[8,2,32,1280]{3,2,1,0:T(8,128)(2,1)} %bitcast.2, bf16[64,64,160]{2,1,0:T(8,128)(2,1)} %e_in.1), custom_call_target="tpu_custom_call" | custom-call | flops 4000000000 | bytes 10000000 | tf_op jit(solution)/shard_map/pallas_call | solution.py:464
  121.4 1.3 %copy.7 = f32[8,32]{1,0:T(8,128)} copy(f32[8,32]{1,0:T(8,128)} %shard_map.55) | data formatting | bytes 2048

commit v4 on v3

--- a/solution.py
+++ b/solution.py
@@ -11,7 +11,7 @@
 BF16 = jnp.bfloat16
 F32 = jnp.float32
 GROUPS = 8
-STEPS = 27
+STEPS = 26
 LATE = 256
 UNITS = 10
 HALF = 640
@@ -390,20 +390,20 @@
         def _(i=i + 0):
             stage4(i)
 
+        on, i = pick(t, (7, 9, 12, 14, 17, 19, 22, 24))
+
+        @pl.when(on)
+        def _(i=i + 0):
+            a_collect(i)
+
         on, i = pick(t, (8, 10, 13, 15, 18, 20, 23, 25))
-
-        @pl.when(on)
-        def _(i=i + 0):
-            a_collect(i)
-
-        on, i = pick(t, (9, 11, 14, 16, 19, 21, 24, 26))
 
         @pl.when(on)
         def _(i=i + 0):
             a_ready(i)
             example_grads(i)
 
-        on, i = pick(t, (16, 17, 18, 19, 20))
+        on, i = pick(t, (15, 16, 17, 18, 19))
 
         @pl.when(on)
         def _(i=i + 0):

time: 123 us -> 122 us (level)
  no operation moved by 1% of the time
where the time goes in v4:
time: 122 us
  Pallas kernels  121 us (99%)
  local copies, waits for them, and re-layouts  1.28 us (1%)
    pallas_call x1, Pallas kernels, per_device(): pl.pallas_call(kernel, out_shape=jax.ShapeDtypeStruct((8, 32), F32), in_s...  121 us

profile of v4, /device:TPU:1, one launch (start us, length us, event | category | flops | bytes accessed | tf_op | source)
XLA Modules:
  0.0 122.0 jit_solution(1574006898121999179)
XLA Ops:
  0.0 120.7 %shard_map.55 = f32[8,32]{1,0:T(8,128)} custom-call(bf16[160,1280]{1,0:T(8,128)(2,1)} %bitcast.3, bf16[1280,1280]{1,0:T(8,128)(2,1)} %iinv_in.1, bf16[1280,1280]{1,0:T(8,128)(2,1)} %oinv_in.1, bf16[8,2,32,1280]{3,2,1,0:T(8,128)(2,1)} %bitcast.2, bf16[64,64,160]{2,1,0:T(8,128)(2,1)} %e_in.1), custom_call_target="tpu_custom_call" | custom-call | flops 4000000000 | bytes 10000000 | tf_op jit(solution)/shard_map/pallas_call | solution.py:464
  120.7 1.3 %copy.7 = f32[8,32]{1,0:T(8,128)} copy(f32[8,32]{1,0:T(8,128)} %shard_map.55) | data formatting | bytes 2048

commit v5 on v4

--- a/solution.py
+++ b/solution.py
@@ -11,7 +11,7 @@
 BF16 = jnp.bfloat16
 F32 = jnp.float32
 GROUPS = 8
-STEPS = 26
+STEPS = 30
 LATE = 256
 UNITS = 10
 HALF = 640
@@ -348,62 +348,62 @@
         return carry
 
     def step(t, carry):
-        on, i = pick(t, (2, 4, 7, 9, 12, 14, 17, 19))
+        on, i = pick(t, (2, 5, 8, 11, 14, 17, 20, 23))
 
         @pl.when(on)
         def _(i=i + 0):
             a_pass(i)
 
-        on, i = pick(t, (2, 4, 7, 9, 12, 14))
+        on, i = pick(t, (2, 5, 8, 11, 14, 17))
 
         @pl.when(on)
         def _(i=i + 2):
             a_send(i)
 
-        on, i = pick(t, (3, 6, 9, 12))
+        on, i = pick(t, (4, 8, 12, 16))
 
         @pl.when(on)
         def _(i=i + 1):
             stage1(i)
 
-        on, i = pick(t, (0, 3))
+        on, i = pick(t, (0, 4))
 
         @pl.when(on)
         def _(i=i + 3):
             stage0(i)
 
-        on, i = pick(t, (4, 7, 10, 13, 16))
+        on, i = pick(t, (5, 9, 13, 17, 21))
 
         @pl.when(on)
         def _(i=i + 0):
             stage2(i)
 
-        on, i = pick(t, (8, 11, 14, 17, 18))
+        on, i = pick(t, (10, 14, 18, 22, 23))
 
         @pl.when(on)
         def _(i=i + 0):
             stage3(i)
 
-        on, i = pick(t, (11, 14, 17, 18, 19))
+        on, i = pick(t, (14, 18, 22, 23, 24))
 
         @pl.when(on)
         def _(i=i + 0):
             stage4(i)
 
-        on, i = pick(t, (7, 9, 12, 14, 17, 19, 22, 24))
+        on, i = pick(t, (7, 10, 13, 16, 19, 22, 25, 28))
 
         @pl.when(on)
         def _(i=i + 0):
             a_collect(i)
 
-        on, i = pick(t, (8, 10, 13, 15, 18, 20, 23, 25))
+        on, i = pick(t, (8, 11, 14, 17, 20, 23, 26, 29))
 
         @pl.when(on)
         def _(i=i + 0):
             a_ready(i)
             example_grads(i)
 
-        on, i = pick(t, (15, 16, 17, 18, 19))
+        on, i = pick(t, (17, 18, 22, 23, 24))
 
         @pl.when(on)
         def _(i=i + 0):

time: 122 us -> 122 us (level)
  no operation moved by 1% of the time
where the time goes in v5:
time: 122 us
  Pallas kernels  121 us (99%)
  local copies, waits for them, and re-layouts  1.28 us (1%)
    pallas_call x1, Pallas kernels, per_device(): pl.pallas_call(kernel, out_shape=jax.ShapeDtypeStruct((8, 32), F32), in_s...  121 us

profile of v5, /device:TPU:1, one launch (start us, length us, event | category | flops | bytes accessed | tf_op | source)
XLA Modules:
  0.0 122.0 jit_solution(1669137658580002235)
XLA Ops:
  0.0 120.7 %shard_map.55 = f32[8,32]{1,0:T(8,128)} custom-call(bf16[160,1280]{1,0:T(8,128)(2,1)} %bitcast.3, bf16[1280,1280]{1,0:T(8,128)(2,1)} %iinv_in.1, bf16[1280,1280]{1,0:T(8,128)(2,1)} %oinv_in.1, bf16[8,2,32,1280]{3,2,1,0:T(8,128)(2,1)} %bitcast.2, bf16[64,64,160]{2,1,0:T(8,128)(2,1)} %e_in.1), custom_call_target="tpu_custom_call" | custom-call | flops 4000000000 | bytes 10000000 | tf_op jit(solution)/shard_map/pallas_call | solution.py:464
  120.7 1.3 %copy.7 = f32[8,32]{1,0:T(8,128)} copy(f32[8,32]{1,0:T(8,128)} %shard_map.55) | data formatting | bytes 2048
